TPU v7x, 1024 devices: a whole 4x4x32 slice. The times are simulated.
1024 devices in a mesh: dp: 64 (over z, y_lo), node: 16 (over y_hi, x, core).
Axes of the slice: x: 4, y: 4 (y_hi: 2, y_lo: 2; y = y_hi * 2 + y_lo), z: 32, core: 2. Of those that a mesh axis runs over, the one named last changes fastest.
Arguments:
- x_this: bfloat16 [64, 2048, 4096], P('dp', 'node'), may hold values from -6 to 6
- grad_values: bfloat16 [64, 2048, 512], P('dp', 'node'), may hold values from -0.046875 to 0.046875
- x_lower: bfloat16 [64, 2048, 4096], P('dp', 'node'), may hold values from -6 to 6
- norm_gain: float32 [4096], replicated, may hold values from 0.1 to 1.9
- weight_lower: bfloat16 [4096, 512], P('node'), may hold values from -0.09375 to 0.09375
- segment_ids: int32 [64, 2048], P('dp', 'node'), may hold values from 0 to 7, never falling along the last dimension, each value on 1 to 1024 neighbouring positions
Outputs:
- grad_weight: float32 [4096, 512], P('node', 'dp')
- keys_lower: bfloat16 [64, 2048, 512], P('dp', 'node')
Inputs may be any that keep to these rules, and one draw needn't show every extreme that they name: `segment_ids`: document ids never fall along a sequence, start at 0, and each of the 8 documents holds 1 to 1024 tokens.
All inputs are finite; a program needn't handle non-finite values.
Results may differ from a plain program's by a relative error of at most 0.015.
Values may be sent and summed in bfloat16 or wider, within the bound.
A program may use at most 32 MiB of HBM per device.

v0:
```python
import jax
import jax.numpy as jnp
from jax import lax
from jax.sharding import PartitionSpec as P

KV_HEADS = 4
HEAD_DIM = 128


epsilon = 1e-05


def passed_along(block, axis, distance):
    devices = range(lax.axis_size(axis))
    route = [(i - distance, i) for i in devices if i - distance in devices]
    return lax.ppermute(block, axis, route)


def prefix(value, axis, join, neutral):
    count, mine = (lax.axis_size(axis), lax.axis_index(axis))
    pieces = lax.all_gather(value, axis)
    total = jnp.full_like(value, 0) + jnp.asarray(neutral, value.dtype)

    def step(position, total):
        longer = join(total, pieces[position])
        return jnp.where(position < mine, longer, total)

    return lax.fori_loop(0, count - 1, step, total)


def rotate_keys(raw_keys, positions):
    half_size = HEAD_DIM // 2
    heads = raw_keys.reshape(raw_keys.shape[0], KV_HEADS, HEAD_DIM)
    frequency = 500000.0 ** (-(jnp.arange(half_size, dtype=jnp.float32) * 2.0 / HEAD_DIM))
    angle = positions.astype(jnp.float32)[:, None] * frequency[None, :]
    cosine = jnp.cos(angle)[:, None, :]
    sine = jnp.sin(angle)[:, None, :]
    first_half = heads[:, :, :half_size]
    second_half = heads[:, :, half_size:]
    turned = jnp.concatenate(
        [first_half * cosine - second_half * sine, second_half * cosine + first_half * sine], axis=2
    )
    return turned.reshape(raw_keys.shape[0], KV_HEADS * HEAD_DIM)


def on_device(x_this, grad_values, x_lower, norm_gain, weight_lower, segment_ids):
    tok_rows = x_lower.shape[1]
    lower_f32 = x_lower[0].astype(jnp.float32)
    mean_sq = jnp.mean(lower_f32 * lower_f32, axis=1, keepdims=True)
    normed = (lower_f32 * lax.rsqrt(mean_sq + epsilon) * norm_gain[None, :]).astype(jnp.bfloat16)
    whole_weight = lax.all_gather(weight_lower, "node", axis=0, tiled=True)
    raw_keys = jnp.dot(normed, whole_weight, preferred_element_type=jnp.float32)
    doc_ids = segment_ids[0]
    my_index = lax.axis_index("node")
    local_steps = jnp.arange(tok_rows, dtype=jnp.int32)
    steps_here = my_index * tok_rows + local_steps
    inner_before = jnp.concatenate([doc_ids[:1], doc_ids[:-1]])
    inner_marks = jnp.where(doc_ids != inner_before, steps_here, jnp.int32(0))
    before_last = passed_along(doc_ids[-1:], "node", 1)
    first_mark = jnp.where(doc_ids[0] != before_last[0], steps_here[0], jnp.int32(0))
    marks = jnp.where(local_steps == 0, first_mark, inner_marks)
    summary = jnp.max(marks, keepdims=True)
    earlier = prefix(summary, "node", jnp.maximum, jnp.zeros((1,), jnp.int32))
    starts = jnp.maximum(earlier[0], lax.cummax(marks, axis=0))
    positions = steps_here - starts
    keys_lower = rotate_keys(raw_keys, positions).astype(jnp.bfloat16)[None]
    inputs_here = x_this[0]
    grads_here = grad_values[0]
    grad_term = lax.dot_general(
        inputs_here, grads_here, (((0,), (0,)), ((), ())), preferred_element_type=jnp.float32
    )
    node_sum = lax.psum_scatter(
        grad_term.astype(jnp.bfloat16), "node", scatter_dimension=0, tiled=True
    ).astype(jnp.float32)
    grad_weight = lax.psum_scatter(node_sum, "dp", scatter_dimension=1, tiled=True)
    return (grad_weight, keys_lower)


def solution(mesh):
    return jax.shard_map(
        on_device,
        mesh=mesh,
        in_specs=(
            P("dp", "node", None),
            P("dp", "node", None),
            P("dp", "node", None),
            P(),
            P("node", None),
            P("dp", "node"),
        ),
        out_specs=(P("node", "dp"), P("dp", "node", None)),
        check_vma=False,
    )
```

profile of v0, /device:TPU:16, one launch (start us, length us, event | category | flops | bytes accessed | tf_op | source)
XLA Modules:
  0.0 527.5 jit_solution(5908222053946122274)
XLA Ops:
  7.2 0.0 copy-start
  7.2 0.0 reduce-scatter.5.cloned.1.call-start
  7.2 1.2 copy-done
  8.4 4.2 convolution_convert_fusion
  12.5 0.0 copy-start.2
  12.5 0.0 copy-start.1
  12.6 0.0 reduce-scatter.5.cloned.1.call-update
  12.6 0.0 all-gather.2.cloned.1.call-start
  12.6 0.7 all-gather.2.cloned.1.call-update
  13.3 0.0 reduce-scatter.7.cloned.1.call-start
  13.4 0.0 copy-done.2
  13.4 0.6 fusion.11
  14.0 1.9 collective-permute-start
  15.9 1.2 dynamic-slice
  17.1 0.0 copy-done.1
  17.2 0.3 fusion
  17.5 5.2 collective-permute-done
  24.0 0.7 compare_select_fusion.1
  24.7 0.1 copy.20
  24.8 0.2 reduce-window.8
  25.0 1.3 fusion.10
  26.3 1.3 dynamic-update-slice
  27.6 15.0 %all-reduce = s32[16]{0:T(128)S(1)} all-reduce(s32[16]{0:T(128)S(1)} %dynamic-update-slice), channel_id=1, replica_groups=mesh['dp'=64,'node'=16] {'node'}, use_global_device_ids=true, to_apply=%add | all-reduce | flops 16 | bytes 128
  42.6 19.0 %while.13 = (s32[]{:T(128)}, s32[1]{0:T(128)}, s32[]{:T(128)}, s32[16,1]{0,1:T(1,128)S(1)}, s32[]{:T(128)}) while((s32[]{:T(128)}, s32[1]{0:T(128)}, s32[]{:T(128)}, s32[16,1]{0,1:T(1,128)S(1)}, s32[]{:T(128)}) %tuple.48), condition=%wide.region_5.6_spmd, body=%wide.region_4.5_spmd.sunk | while | flops 5 | bytes 115 | solution.py:28
  42.7 0.6 constant_dynamic-slice_fusion.2
  43.9 0.6 constant_dynamic-slice_fusion.2
  45.2 0.6 constant_dynamic-slice_fusion.2
  46.4 0.6 constant_dynamic-slice_fusion.2
  47.7 0.6 constant_dynamic-slice_fusion.2
  49.0 0.6 constant_dynamic-slice_fusion.2
  50.2 0.6 constant_dynamic-slice_fusion.2
  51.5 0.6 constant_dynamic-slice_fusion.2
  52.8 0.6 constant_dynamic-slice_fusion.2
  54.0 0.6 constant_dynamic-slice_fusion.2
  55.3 0.6 constant_dynamic-slice_fusion.2
  56.6 0.6 constant_dynamic-slice_fusion.2
  57.8 0.6 constant_dynamic-slice_fusion.2
  59.1 0.6 constant_dynamic-slice_fusion.2
  60.4 0.6 constant_dynamic-slice_fusion.2
  61.6 0.1 maximum_reduce_fusion
  61.7 93.3 %reduce-scatter.5.cloned.1.call-done = bf16[256,512]{1,0:T(8,128)(2,1)} async-done(((bf16[4096,512]{1,0:T(8,128)(2,1)}), bf16[256,512]{1,0:T(8,128)(2,1)}) %reduce-scatter.5.cloned.1.call-update) | async-done | bytes 262160 | tf_op jit(solution)/shard_map/reduce_scatter | solution.py:72
  155.0 1.9 copy.23
  156.9 0.0 reduce-scatter.7.cloned.1.call-update
  157.0 0.2 multiply_cosine_fusion
  157.2 92.7 %all-gather.2.cloned.1.call-done = bf16[4096,512]{1,0:T(8,128)(2,1)} async-done(((bf16[256,512]{1,0:T(8,128)(2,1)}), bf16[4096,512]{1,0:T(8,128)(2,1)}) %all-gather.2.cloned.1.call-update) | async-done | bytes 4194320 | tf_op jit(solution)/shard_map/all_gather | solution.py:51
  249.9 0.0 copy-start.3
  249.9 6.5 %copy.18 = bf16[512,4096]{1,0:T(8,128)(2,1)} copy(bf16[512,4096]{0,1:T(8,128)(2,1)} %bitcast.43) | data formatting | bytes 8388608 | tf_op jit(solution)/shard_map/dot_general | solution.py:52
  256.3 0.0 copy-done.3
  256.3 3.5 fusion.4
  259.9 0.8 copy.22
  260.7 260.3 %reduce-scatter.7.cloned.1.call-done = f32[8,256]{1,0:T(8,128)} async-done(((f32[512,256]{1,0:T(8,128)}), f32[8,256]{1,0:T(8,128)}) %reduce-scatter.7.cloned.1.call-update) | async-done | bytes 8208
  (8 shorter events, 0.1 us)
Async XLA Ops:
  7.2 1.2 copy-start
  7.2 147.8 %reduce-scatter.5.cloned.1.call-start = ((), (), s32[]{:S(2)}) async-start(), calls=%async_computation.2 | async-start | bytes 4456448 | tf_op jit(solution)/shard_map/reduce_scatter | solution.py:72
  12.5 0.8 copy-start.2
  12.5 4.6 copy-start.1
  12.6 237.3 %all-gather.2.cloned.1.call-start = ((), (), s32[]{:S(2)}) async-start(), calls=%async_computation.3 | async-start | bytes 4456448 | tf_op jit(solution)/shard_map/all_gather | solution.py:51
  13.3 507.7 %reduce-scatter.7.cloned.1.call-start = ((), (), s32[]{:S(2)}) async-start(), calls=%async_computation.4 | async-start | bytes 532480
  14.0 8.7 %collective-permute-start = (s32[1]{0:T(128)}, s32[1]{0:T(128)}, u32[]{:S(2)}, u32[]{:S(2)}) collective-permute-start(s32[1]{0:T(128)} %bitcast.9), channel_id=1, source_target_pairs={{0,1},{1,2},{2,3},{3,4},{4,5},{5,6},{6,7},{7,8},{8,9},{9,10},{10,1... | collective-permute-start | bytes 20 | tf_op jit(solution)/shard_map/ppermute | solution.py:16
  249.9 6.5 %copy-start.3 = (f32[4096]{0:T(1024)S(1)}, f32[4096]{0:T(1024)}, u32[]{:S(2)}) copy-start(f32[4096]{0:T(1024)} %param.11) | copy-start | bytes 49156
Sparse Core Ops, SparseCore 0:
  14.1 140.8 reduce-scatter.4
  160.3 89.5 all-gather.1
  254.2 266.7 reduce-scatter.6
where the time goes:
time: 528 us
  waiting for transfers between devices  452 us (86%)
  local copies, waits for them, and re-layouts  22.4 us (4%)
  between operations  15.2 us (3%)
  blocking collectives  15 us (3%)
  loops' own time  10.2 us (2%)
  matrix products  7.66 us (1%)
    unnamed x4, waiting for transfers between devices  261 us
    reduce_scatter x1, waiting for transfers between devices, on_device(): lax.psum_scatter(grad_term.astype(jnp.bfloat16), 'node', scatter_dimensio...  93.3 us
    all_gather x1, waiting for transfers between devices, on_device(): whole_weight = lax.all_gather(weight_lower, 'node', axis=0, tiled=True)  92.7 us
    unnamed x1, blocking collectives  15 us
  transfers between devices with their start and end apart: 4, of which 4 were waited for; matrix products, arithmetic and copies ran while one was open for 5% of the time, Pallas kernels for 0%

commit v1 on v0

v1 whole, which is shorter than its diff:
```python
import functools
import math

import jax
import jax.numpy as jnp
import numpy as np
from jax import lax
from jax.experimental import pallas as pl
from jax.experimental.pallas import tpu as pltpu
from jax.sharding import PartitionSpec as P

EPS = 1e-05
MESH = pl.DeviceIdType.MESH
F32 = jnp.float32
BF16 = jnp.bfloat16
N_SEM = 72
ORDER = (2, 1, 3, 0)
ROUTES = (("x", 1, 3), ("x", 3, 1), ("y", 1, 3), ("y", 3, 1))


def flip(v, mask):
    if mask == 0:
        return v
    if mask == 1:
        return v + 1 - 2 * lax.rem(v, 2)
    if mask == 2:
        return lax.rem(v + 2, 4)
    return 3 - v


def kernel(
    x_hbm, g_hbm, low_hbm, gain_hbm, w_hbm, ids_hbm, freq_hbm,
    grad_ref, keys_ref,
    x_v, g_v, low_v, gain_v, w_v, ids_v, freq_v,
    gt_f, gt2, c_send, c_recv, s_buf, r1, r2, r3, r4, z1, z2, zs,
    wg, normed, acc, kr, cs, cr,
    local_sem, send_sem, recv_sem,
):
    dp = lax.axis_index("dp")
    node = lax.axis_index("node")
    z, yl = lax.div(dp, 2), lax.rem(dp, 2)
    yh = lax.div(node, 8)
    x = lax.rem(lax.div(node, 2), 4)
    c = lax.rem(node, 2)
    y = yh * 2 + yl
    par = lax.rem(z, 2)

    def dev(jx=0, jy=0, dz=0, other=False):
        ty = flip(y, jy)
        tz = lax.rem(z + dz + 32, 32)
        tc = 1 - c if other else c
        return (tz * 2 + lax.rem(ty, 2), lax.div(ty, 2) * 8 + flip(x, jx) * 2 + tc)

    sent = []

    def send(src, dst, device):
        i = len(sent)
        copy = pltpu.make_async_remote_copy(
            src_ref=src, dst_ref=dst, send_sem=send_sem.at[i], recv_sem=recv_sem.at[i],
            device_id=device, device_id_type=MESH,
        )
        copy.start()
        sent.append(copy)
        return copy

    loads = []
    for src, dst in (
        (g_hbm, g_v), (x_hbm, x_v), (w_hbm, w_v), (ids_hbm, ids_v),
        (low_hbm, low_v), (gain_hbm, gain_v), (freq_hbm, freq_v),
    ):
        copy = pltpu.make_async_copy(src, dst, local_sem.at[len(loads)])
        copy.start()
        loads.append(copy)
    ld_g, ld_x, ld_w, ld_ids, ld_low, ld_gain, ld_freq = loads

    barrier = pltpu.get_barrier_semaphore()
    greet = [dev(other=True), dev(jx=1), dev(jx=3), dev(jy=1), dev(jy=3), dev(jy=2)]
    greet += [dev(dz=1), dev(dz=-1), dev(dz=2), dev(dz=-2)]
    greet += [dev(dz=4 * a) for a in range(1, 8)]
    for device in greet:
        pl.semaphore_signal(barrier, inc=1, device_id=device, device_id_type=MESH)

    ld_g.wait()
    gt_f[...] = g_v[0].astype(F32).T.reshape(32, 2, 8, 128)
    mine_first = jnp.concatenate([gt_f[:, yl], gt_f[:, 1 - yl]], axis=1).astype(BF16).reshape(512, 128)
    gt2[0:512, :] = mine_first
    gt2[512:1024, :] = mine_first
    g_rows = pl.ds(pl.multiple_of(z * 16, 16), 512)

    def term(jx, jyh, core):
        owner = (yh + jyh - 2 * yh * jyh) * 8 + flip(x, jx) * 2 + core
        lanes = pl.ds(pl.multiple_of(owner * 256, 256), 256)
        t = jnp.dot(gt2[g_rows, :], x_v[0, :, lanes], preferred_element_type=F32)
        t = t.reshape(8, 4, 2, 8, 256)

        def piece(b, jl):
            part = t[:, b, jl]
            return jnp.concatenate([part[:, :, :128], part[:, :, 128:]], axis=1)

        return piece

    ld_x.wait()
    ld_ids.wait()
    ids_row = jnp.broadcast_to(ids_v[...].astype(F32), (128, 128))
    sub = lax.broadcasted_iota(jnp.int32, (128, 128), 0)
    lane = lax.broadcasted_iota(jnp.int32, (128, 128), 1)
    id_col = jnp.sum(jnp.where(sub == lane, ids_row, 0.0), axis=1, keepdims=True)
    lane_f = lane.astype(F32)
    count = jnp.sum(jnp.where(id_col < lane_f, 1.0, 0.0), axis=0, keepdims=True)
    cs[0] = jnp.broadcast_to(count, (8, 128))

    c_copies = {}
    w0 = None
    for step, jx in enumerate(ORDER):
        for jyh in range(2):
            piece = term(jx, jyh, 1 - c)
            for b in range(4):
                for jl in range(2):
                    c_send[jx, jyh, b, jl] = piece(b, jl).astype(BF16)
            if step == 0 and jyh == 0:
                pl.semaphore_wait(barrier, len(greet))
                cc = [send(cs.at[0], cr.at[0], dev(other=True))]
                ld_w.wait()
                rows = pl.ds(pl.multiple_of(par * 128, 128), 128)
                away = pl.ds(pl.multiple_of((1 - c) * 256, 256), 256)
                here = pl.ds(pl.multiple_of(c * 256, 256), 256)
                wg[0, 0, 0, c] = w_v[rows, here]
                kr_w = w_v.at[rows, away]
                w0 = send(kr_w, wg.at[0, 0, 0, c], dev(other=True))
            c_copies[jx, jyh] = send(c_send.at[jx, jyh], c_recv.at[jx, jyh], dev(other=True))

    w0.wait_recv()
    w1a = send(wg.at[0, 0, 0], wg.at[0, 0, 1], dev(jx=1))
    w1b = send(wg.at[0, 0, 0], wg.at[0, 0, 3], dev(jx=3))

    r1_copies = {b: [] for b in range(4)}
    for jx in ORDER:
        for jyh in range(2):
            piece = term(jx, jyh, c)
            c_copies[jx, jyh].wait_recv()
            for b in range(4):
                for jl in range(2):
                    jy = jyh * 2 + jl
                    total = (piece(b, jl) + c_recv[jx, jyh, b, jl].astype(F32)).astype(BF16)
                    if b < 2:
                        s_buf[b, jx, jy] = total
                    else:
                        s_buf[b, jy, jx] = total
        for b, (axis, m1, m2) in enumerate(ROUTES):
            low = min(m1, 2)
            if axis == "x":
                if jx in (m1, 2):
                    r1_copies[b].append(send(s_buf.at[b, jx], r1.at[b, jx - low], dev(jx=m1)))
            else:
                r1_copies[b].append(
                    send(s_buf.at[b, low:low + 2, jx], r1.at[b, :, jx], dev(jy=m1))
                )

    cc[0].wait_recv()
    cs[1] = cs[0] + cr[0]
    cc.append(send(cs.at[1], cr.at[1], dev(jx=1)))

    w1a.wait_recv()
    w1b.wait_recv()
    w2a = send(wg.at[0, 0, 3, 0], wg.at[0, 0, 2, 0], dev(jx=1))
    w2b = send(wg.at[0, 0, 1, 1], wg.at[0, 0, 2, 1], dev(jx=3))

    ld_low.wait()
    ld_gain.wait()
    gain = gain_v[...]

    def norm_rows(i, carry):
        rows = pl.ds(pl.multiple_of(i * 16, 16), 16)
        v = low_v[0, rows, :].astype(F32)
        mean_sq = jnp.sum(v * v, axis=1, keepdims=True) * (1.0 / 4096)
        normed[rows, :] = (v * lax.rsqrt(mean_sq + EPS) * gain).astype(BF16)
        return carry

    lax.fori_loop(0, 8, norm_rows, 0)
    nb = send(normed.at[0:128], normed.at[128:256], dev(other=True))

    w2a.wait_recv()
    w2b.wait_recv()
    w3 = send(wg.at[0, 0, :, 1 - yl], wg.at[0, 1, :, 1 - yl], dev(jy=3))
    w5 = [
        send(wg.at[0, 0, :, 0], wg.at[1, 0, :, 0], dev(dz=1)),
        send(wg.at[0, 0, :, 1], wg.at[1, 0, :, 1], dev(dz=-1)),
    ]

    cc[1].wait_recv()
    cs[2] = cs[1] + cr[1]
    cc.append(send(cs.at[2], cr.at[2], dev(jx=3)))

    def to(axis, mask):
        return dev(jx=mask) if axis == "x" else dev(jy=mask)

    r2_copies = []
    for b, (axis, m1, m2) in enumerate(ROUTES):
        for copy in r1_copies[b]:
            copy.wait_recv()
        low = min(m1, 2)
        s_buf[b, m2] = s_buf[b, m2] + r1[b, 2 - low]
        r2_copies.append(send(s_buf.at[b, m2], r2.at[b], to(axis, m2)))
        s_buf[b, 0] = s_buf[b, 0] + r1[b, m1 - low]

    w3.wait_recv()
    w4 = send(wg.at[0, 1, :, yl], wg.at[0, 1, :, yl], dev(jy=1))
    w5.append(send(wg.at[0, 1, :, yl], wg.at[1, 1, :, yl], dev(dz=1 - 2 * yl)))

    r3_copies = []
    for b, (axis, m1, m2) in enumerate(ROUTES):
        r2_copies[b].wait_recv()
        other = "y" if axis == "x" else "x"
        low = min(m1, 2)
        s_buf[b, 0] = s_buf[b, 0] + r2[b]
        r3_copies.append(send(s_buf.at[b, 0, low:low + 2], r3.at[b], to(other, m1)))

    cc[2].wait_recv()
    cs[3] = cs[2] + cr[2]
    cc.append(send(cs.at[3], cr.at[3], dev(jy=2)))

    r4_copies = []
    for b, (axis, m1, m2) in enumerate(ROUTES):
        r3_copies[b].wait_recv()
        other = "y" if axis == "x" else "x"
        low = min(m1, 2)
        s_buf[b, 0, m2] = s_buf[b, 0, m2] + r3[b, 2 - low]
        r4_copies.append(send(s_buf.at[b, 0, m2], r4.at[b], to(other, m2)))
        s_buf[b, 0, 0] = s_buf[b, 0, 0] + r3[b, m1 - low]

    w4.wait_recv()
    w5.append(send(wg.at[0, 1, :, 1 - yl], wg.at[1, 1, :, 1 - yl], dev(dz=2 * yl - 1)))

    z1_copies = []
    for b in (1, 2, 3):
        r4_copies[b].wait_recv()
        s_buf[b, 0, 0] = s_buf[b, 0, 0] + r4[b]
        z1_copies.append(send(s_buf.at[b, 0, 0], z1.at[b - 1], dev(dz=(0, 1, 2, -1)[b])))
    r4_copies[0].wait_recv()
    kept = s_buf[0, 0, 0].astype(F32) + r4[0].astype(F32)

    nb.wait_recv()

    def project(jp):
        for jyh in range(2):
            for jx in range(4):
                owner = (yh + jyh - 2 * yh * jyh) * 8 + flip(x, jx) * 2
                half = par if jp == 0 else 1 - par
                lhs = jnp.concatenate(
                    [
                        normed[:, pl.ds(pl.multiple_of((owner + s) * 256 + half * 128, 128), 128)]
                        for s in range(2)
                    ],
                    axis=1,
                )
                part = jnp.dot(lhs, wg[jp, jyh, jx].reshape(256, 256), preferred_element_type=F32)
                if jp == 0 and jyh == 0 and jx == 0:
                    acc[...] = part
                else:
                    acc[...] += part

    project(0)

    for copy in z1_copies:
        copy.wait_recv()
    kept = kept + z1[0].astype(F32) + z1[1].astype(F32)
    late = z1[2].astype(F32)
    kept = kept + jnp.concatenate([late[7:8], late[0:7]], axis=0)
    zs[...] = kept.astype(BF16)
    z2_copies = [send(zs.at[a], z2.at[a - 1], dev(dz=4 * a)) for a in range(1, 8)]

    for copy in w5:
        copy.wait_recv()
    project(1)
    kx = send(acc.at[128:256], kr, dev(other=True))

    cc[3].wait_recv()
    counts = (cs[3] + cr[3])[0:1]
    start = jnp.sum(jnp.where(lane_f == id_col, counts, 0.0), axis=1, keepdims=True)
    first_token = (node * 128).astype(F32)
    token = lax.broadcasted_iota(jnp.int32, (128, 1), 0).astype(F32)
    positions = token + first_token - start
    ld_freq.wait()
    angle = positions * freq_v[...]
    cosine = jnp.cos(angle)
    sine = jnp.where(lane < 64, -1.0, 1.0) * jnp.sin(angle)

    def rotate(source, half):
        for h in range(2):
            k = source[0:128, h * 128:(h + 1) * 128]
            turned = k * cosine + pltpu.roll(k, 64, 1) * sine
            lanes = pl.ds(pl.multiple_of(half * 256 + h * 128, 128), 128)
            keys_ref[:, lanes] = turned.astype(BF16)

    rotate(acc, c)
    kx.wait_recv()
    rotate(kr, 1 - c)

    total = kept[0]
    for a in range(7):
        z2_copies[a].wait_recv()
        total = total + z2[a].astype(F32)
    grad_ref[...] = total

    for copy in sent:
        copy.wait_send()


def fused(x_this, grad_values, x_lower, gain, weight_lower, ids, freq):
    tiles = (8, 16, 128)
    anywhere = pl.BlockSpec(memory_space=pl.ANY)
    vmem = pl.BlockSpec(memory_space=pltpu.VMEM)
    return pl.pallas_call(
        kernel,
        out_shape=(
            jax.ShapeDtypeStruct((16, 128), F32),
            jax.ShapeDtypeStruct((128, 512), BF16),
        ),
        in_specs=[anywhere] * 7,
        out_specs=(vmem, vmem),
        scratch_shapes=[
            pltpu.VMEM((1, 128, 4096), BF16),
            pltpu.VMEM((1, 128, 512), BF16),
            pltpu.VMEM((1, 128, 4096), BF16),
            pltpu.VMEM((1, 4096), F32),
            pltpu.VMEM((256, 512), BF16),
            pltpu.VMEM((1, 128), jnp.int32),
            pltpu.VMEM((1, 128), F32),
            pltpu.VMEM((32, 2, 8, 128), F32),
            pltpu.VMEM((1024, 128), BF16),
            pltpu.VMEM((4, 2, 4, 2) + tiles, BF16),
            pltpu.VMEM((4, 2, 4, 2) + tiles, BF16),
            pltpu.VMEM((4, 4, 4) + tiles, BF16),
            pltpu.VMEM((4, 2, 4) + tiles, BF16),
            pltpu.VMEM((4, 4) + tiles, BF16),
            pltpu.VMEM((4, 2) + tiles, BF16),
            pltpu.VMEM((4,) + tiles, BF16),
            pltpu.VMEM((3,) + tiles, BF16),
            pltpu.VMEM((7, 16, 128), BF16),
            pltpu.VMEM(tiles, BF16),
            pltpu.VMEM((2, 2, 4, 2, 128, 256), BF16),
            pltpu.VMEM((256, 4096), BF16),
            pltpu.VMEM((256, 256), F32),
            pltpu.VMEM((128, 256), F32),
            pltpu.VMEM((4, 8, 128), F32),
            pltpu.VMEM((4, 8, 128), F32),
            pltpu.SemaphoreType.DMA((7,)),
            pltpu.SemaphoreType.DMA((N_SEM,)),
            pltpu.SemaphoreType.DMA((N_SEM,)),
        ],
        compiler_params=pltpu.CompilerParams(
            collective_id=0, has_side_effects=True, vmem_limit_bytes=40 * 1024 * 1024
        ),
        cost_estimate=pl.CostEstimate(
            flops=2 * 2 * 128 * 4096 * 512, bytes_accessed=4 * 1024 * 1024, transcendentals=32768
        ),
    )(x_this, grad_values, x_lower, gain, weight_lower, ids, freq)


def on_device(x_this, grad_values, x_lower, norm_gain, weight_lower, segment_ids):
    exponent = np.arange(128) % 64 * 2.0 / 128
    freq = jnp.asarray((500000.0 ** (-exponent)).astype(np.float32)[None])
    grad, keys = fused(
        x_this, grad_values, x_lower, norm_gain[None], weight_lower, segment_ids, freq
    )
    grad = grad.reshape(2, 8, 128).transpose(0, 2, 1).reshape(256, 8)
    return (grad, keys[None])


def solution(mesh):
    return jax.shard_map(
        on_device,
        mesh=mesh,
        in_specs=(
            P("dp", "node", None),
            P("dp", "node", None),
            P("dp", "node", None),
            P(),
            P("node", None),
            P("dp", "node"),
        ),
        out_specs=(P("node", "dp"), P("dp", "node", None)),
        check_vma=False,
    )
```

time: 528 us -> 87.5 us (0.17)
  the two profiles are of different devices: /device:TPU:16 before, /device:TPU:8 now
where the time goes in v1:
time: 87.5 us; the launch traced here: 87.2 us
  Pallas kernels  79.6 us (91%)
  local copies, waits for them, and re-layouts  6.93 us (8%)
    pallas_call x1, Pallas kernels, fused(): pl.pallas_call(kernel, out_shape=(jax.ShapeDtypeStruct((16, 128), F32), j...  79.6 us
    unnamed x16, local copies, waits for them, and re-layouts  6.93 us

profile of v1, /device:TPU:8, one launch (start us, length us, event | category | flops | bytes accessed | tf_op | source)
XLA Modules:
  0.0 87.2 jit_solution(11219239698036950942)
XLA Ops:
  0.6 0.0 copy-start.6
  0.6 0.0 copy-start.5
  0.7 0.6 copy-done.6
  1.3 0.0 copy-done.5
  1.3 0.0 copy-start
  1.3 1.2 %copy-done = bf16[1,128,4096]{2,1,0:T(8,128)(2,1)S(1)} copy-done((bf16[1,128,4096]{2,1,0:T(8,128)(2,1)S(1)}, bf16[1,128,4096]{2,1,0:T(8,128)(2,1)}, u32[]{:S(2)}) %copy-start) | copy-done | bytes 1048600
  2.5 0.0 copy-start.1
  2.5 1.2 %copy-done.1 = bf16[1,128,4096]{2,1,0:T(8,128)(2,1)S(1)} copy-done((bf16[1,128,4096]{2,1,0:T(8,128)(2,1)S(1)}, bf16[1,128,4096]{2,1,0:T(8,128)(2,1)}, u32[]{:S(2)}) %copy-start.1) | copy-done | bytes 1048600
  3.8 0.0 copy-start.2
  3.8 0.9 %copy-done.2 = bf16[256,512]{1,0:T(8,128)(2,1)S(1)} copy-done((bf16[256,512]{1,0:T(8,128)(2,1)S(1)}, bf16[256,512]{1,0:T(8,128)(2,1)}, u32[]{:S(2)}) %copy-start.2) | copy-done | bytes 262168
  4.7 0.0 copy-start.3
  4.7 0.9 %copy-done.3 = bf16[1,128,512]{2,1,0:T(8,128)(2,1)S(1)} copy-done((bf16[1,128,512]{2,1,0:T(8,128)(2,1)S(1)}, bf16[1,128,512]{2,1,0:T(8,128)(2,1)}, u32[]{:S(2)}) %copy-start.3) | copy-done | bytes 131096
  5.6 0.0 copy-start.4
  5.6 0.7 copy-done.4
  6.3 79.6 %shard_map.86 = (f32[16,128]{1,0:T(8,128)S(1)}, bf16[128,512]{1,0:T(8,128)(2,1)S(1)}) custom-call(bf16[1,128,4096]{2,1,0:T(8,128)(2,1)S(1)} %copy-done, bf16[1,128,512]{2,1,0:T(8,128)(2,1)S(1)} %copy-done.3, bf16[1,128,4096]{2,1,0:T(8,128)(2,1)S(1)} %copy-done.1, f32[1,4096]{1,0:T(1,128)S(1)} %bitcast.9, bf16[256,512]{1,0:T(8,128)(2,1)S(1)} %copy-done.2, ...), custom_call_target="tpu_custom_call" | custom-call | flops 1073741824 | bytes 4194304 | tf_op jit(solution)/shard_map/pallas_call | solution.py:313
  85.9 0.6 copy.11
  86.5 0.7 copy.12
Async XLA Ops:
  0.6 0.7 copy-start.6
  0.6 0.7 copy-start.5
  1.3 1.2 %copy-start = (bf16[1,128,4096]{2,1,0:T(8,128)(2,1)S(1)}, bf16[1,128,4096]{2,1,0:T(8,128)(2,1)}, u32[]{:S(2)}) copy-start(bf16[1,128,4096]{2,1,0:T(8,128)(2,1)} %x_hbm.1) | copy-start | bytes 3145732
  2.5 1.2 %copy-start.1 = (bf16[1,128,4096]{2,1,0:T(8,128)(2,1)S(1)}, bf16[1,128,4096]{2,1,0:T(8,128)(2,1)}, u32[]{:S(2)}) copy-start(bf16[1,128,4096]{2,1,0:T(8,128)(2,1)} %low_hbm.1) | copy-start | bytes 3145732
  3.8 0.9 %copy-start.2 = (bf16[256,512]{1,0:T(8,128)(2,1)S(1)}, bf16[256,512]{1,0:T(8,128)(2,1)}, u32[]{:S(2)}) copy-start(bf16[256,512]{1,0:T(8,128)(2,1)} %w_hbm.1) | copy-start | bytes 786436
  4.7 0.9 %copy-start.3 = (bf16[1,128,512]{2,1,0:T(8,128)(2,1)S(1)}, bf16[1,128,512]{2,1,0:T(8,128)(2,1)}, u32[]{:S(2)}) copy-start(bf16[1,128,512]{2,1,0:T(8,128)(2,1)} %g_hbm.1) | copy-start | bytes 393220
  5.6 0.7 copy-start.4

commit v2 on v1

v2 whole, which is shorter than its diff:
```python
import functools
import math

import jax
import jax.numpy as jnp
import numpy as np
from jax import lax
from jax.experimental import pallas as pl
from jax.experimental.pallas import tpu as pltpu
from jax.sharding import PartitionSpec as P

EPS = 1e-05
MESH = pl.DeviceIdType.MESH
F32 = jnp.float32
BF16 = jnp.bfloat16
N_SEM = 112
ORDER = (2, 1, 3, 0)
ROUTES = (("x", 1, 3), ("x", 3, 1), ("y", 1, 3), ("y", 3, 1))


def flip(v, mask):
    if mask == 0:
        return v
    if mask == 1:
        return v + 1 - 2 * lax.rem(v, 2)
    if mask == 2:
        return lax.rem(v + 2, 4)
    return 3 - v


def kernel(
    x_hbm, g_hbm, low_hbm, gain_hbm, w_hbm, ids_hbm, freq_hbm,
    grad_ref, keys_ref,
    x_v, g_v, low_v, gain_v, w_v, ids_v, freq_v,
    gt_f, gt2, c_send, c_recv, s_buf, r1, r2, r3, r4, z1, z2, zs,
    wg, normed, acc, kr, cs, cr, trig,
    local_sem, send_sem, recv_sem, far_sem,
):
    dp = lax.axis_index("dp")
    node = lax.axis_index("node")
    z, yl = lax.div(dp, 2), lax.rem(dp, 2)
    yh = lax.div(node, 8)
    x = lax.rem(lax.div(node, 2), 4)
    c = lax.rem(node, 2)
    y = yh * 2 + yl
    par = lax.rem(z, 2)

    def dev(jx=0, jy=0, dz=0, other=False):
        ty = flip(y, jy)
        tz = lax.rem(z + dz + 32, 32)
        tc = 1 - c if other else c
        return (tz * 2 + lax.rem(ty, 2), lax.div(ty, 2) * 8 + flip(x, jx) * 2 + tc)

    sent = []

    def send(src, dst, device):
        i = len(sent)
        copy = pltpu.make_async_remote_copy(
            src_ref=src, dst_ref=dst, send_sem=send_sem.at[i], recv_sem=recv_sem.at[i],
            device_id=device, device_id_type=MESH,
        )
        copy.start()
        sent.append(copy)
        return copy

    loads = []
    for src, dst in (
        (ids_hbm, ids_v), (g_hbm, g_v), (w_hbm, w_v), (x_hbm, x_v),
        (low_hbm, low_v), (gain_hbm, gain_v), (freq_hbm, freq_v),
    ):
        copy = pltpu.make_async_copy(src, dst, local_sem.at[len(loads)])
        copy.start()
        loads.append(copy)
    ld_ids, ld_g, ld_w, ld_x, ld_low, ld_gain, ld_freq = loads

    barrier = pltpu.get_barrier_semaphore()
    greet = [dev(other=True), dev(jx=1), dev(jx=3), dev(jy=1), dev(jy=3), dev(jy=2)]
    greet += [dev(dz=1), dev(dz=-1), dev(dz=2), dev(dz=-2)]
    for device in greet:
        pl.semaphore_signal(barrier, inc=1, device_id=device, device_id_type=MESH)

    ld_ids.wait()
    ids_row = jnp.broadcast_to(ids_v[...].astype(F32), (128, 128))
    sub = lax.broadcasted_iota(jnp.int32, (128, 128), 0)
    lane = lax.broadcasted_iota(jnp.int32, (128, 128), 1)
    id_col = jnp.sum(jnp.where(sub == lane, ids_row, 0.0), axis=1, keepdims=True)
    lane_f = lane.astype(F32)
    count = jnp.sum(jnp.where(id_col < lane_f, 1.0, 0.0), axis=0, keepdims=True)
    cs[0] = jnp.broadcast_to(count, (8, 128))

    ld_g.wait()
    gt_f[...] = g_v[0].astype(F32).T.reshape(32, 2, 8, 128)
    mine_first = jnp.concatenate([gt_f[:, yl], gt_f[:, 1 - yl]], axis=1).astype(BF16).reshape(512, 128)
    gt2[0:512, :] = mine_first
    gt2[512:1024, :] = mine_first
    g_rows = pl.ds(pl.multiple_of(z * 16, 16), 512)

    def term(jx, jyh, core):
        owner = (yh + jyh - 2 * yh * jyh) * 8 + flip(x, jx) * 2 + core
        lanes = pl.ds(pl.multiple_of(owner * 256, 256), 256)
        t = jnp.dot(gt2[g_rows, :], x_v[0, :, lanes], preferred_element_type=F32)
        t = t.reshape(8, 4, 2, 8, 256)

        def piece(b, jl):
            part = t[:, b, jl]
            return jnp.concatenate([part[:, :, :128], part[:, :, 128:]], axis=1)

        return piece

    ld_w.wait()
    rows = pl.ds(pl.multiple_of(par * 128, 128), 128)
    away = pl.ds(pl.multiple_of((1 - c) * 256, 256), 256)
    here = pl.ds(pl.multiple_of(c * 256, 256), 256)
    wg[0, 0, 0, c] = w_v[rows, here]
    pl.semaphore_wait(barrier, len(greet))
    def far_signal(i):
        for side in (1, -1):
            pl.semaphore_signal(
                far_sem.at[i], inc=1, device_id=dev(dz=side * 2 * 2 ** i), device_id_type=MESH
            )

    far_signal(0)
    w0 = send(w_v.at[rows, away], wg.at[0, 0, 0, c], dev(other=True))
    cc = [send(cs.at[0], cr.at[0], dev(other=True))]
    w3, w4, w5 = {}, {}, []

    def spread(jx):
        w3[jx] = send(wg.at[0, 0, jx, 1 - yl], wg.at[0, 1, jx, 1 - yl], dev(jy=3))
        w5.append(send(wg.at[0, 0, jx, 0], wg.at[1, 0, jx, 0], dev(dz=1)))
        w5.append(send(wg.at[0, 0, jx, 1], wg.at[1, 0, jx, 1], dev(dz=-1)))

    def share(jx):
        w3[jx].wait_recv()
        w4[jx] = send(wg.at[0, 1, jx, yl], wg.at[0, 1, jx, yl], dev(jy=1))
        w5.append(send(wg.at[0, 1, jx, yl], wg.at[1, 1, jx, yl], dev(dz=1 - 2 * yl)))

    def pass_on(jx):
        w4[jx].wait_recv()
        w5.append(send(wg.at[0, 1, jx, 1 - yl], wg.at[1, 1, jx, 1 - yl], dev(dz=2 * yl - 1)))

    ld_x.wait()
    c_copies = {}
    r1_copies = {}

    def for_sibling(jx):
        for jyh in (1, 0):
            piece = term(jx, jyh, 1 - c)
            for b in range(4):
                for jl in range(2):
                    c_send[jx, jyh, b, jl] = piece(b, jl).astype(BF16)
            c_copies[jx, jyh] = send(c_send.at[jx, jyh], c_recv.at[jx, jyh], dev(other=True))

    def own(jx):
        for jyh in (1, 0):
            piece = term(jx, jyh, c)
            c_copies[jx, jyh].wait_recv()
            for b in range(4):
                for jl in range(2):
                    jy = jyh * 2 + jl
                    total = (piece(b, jl) + c_recv[jx, jyh, b, jl].astype(F32)).astype(BF16)
                    if b < 2:
                        s_buf[b, jx, jy] = total
                    else:
                        s_buf[b, jy, jx] = total
            pair = slice(jyh * 2, jyh * 2 + 2)
            for b, (axis, m1, m2) in enumerate(ROUTES):
                low = min(m1, 2)
                if axis == "x" and jx in (m1, 2):
                    r1_copies[b, jx, jyh] = send(
                        s_buf.at[b, jx, pair], r1.at[b, jx - low, pair], dev(jx=m1)
                    )
        for b, (axis, m1, m2) in enumerate(ROUTES):
            low = min(m1, 2)
            if axis == "y":
                r1_copies[b, jx] = send(
                    s_buf.at[b, low:low + 2, jx], r1.at[b, :, jx], dev(jy=m1)
                )

    for_sibling(2)
    for_sibling(1)
    w0.wait_recv()
    w1a = send(wg.at[0, 0, 0], wg.at[0, 0, 1], dev(jx=1))
    w1b = send(wg.at[0, 0, 0], wg.at[0, 0, 3], dev(jx=3))
    spread(0)
    own(2)
    for_sibling(3)
    own(1)
    cc[0].wait_recv()
    cs[1] = cs[0] + cr[0]
    cc.append(send(cs.at[1], cr.at[1], dev(jx=1)))
    w1a.wait_recv()
    w1b.wait_recv()
    w2a = send(wg.at[0, 0, 3, 0], wg.at[0, 0, 2, 0], dev(jx=1))
    w2b = send(wg.at[0, 0, 1, 1], wg.at[0, 0, 2, 1], dev(jx=3))
    spread(1)
    spread(3)
    for_sibling(0)
    own(3)
    share(0)
    pl.semaphore_wait(far_sem.at[0], 2)
    far_signal(1)
    own(0)
    cc[1].wait_recv()
    cs[2] = cs[1] + cr[1]
    cc.append(send(cs.at[2], cr.at[2], dev(jx=3)))
    w2a.wait_recv()
    w2b.wait_recv()
    spread(2)
    share(1)
    pass_on(0)
    share(3)

    ld_low.wait()
    ld_gain.wait()
    gain = gain_v[...]

    def norm_rows(i, carry):
        rows = pl.ds(pl.multiple_of(i * 16, 16), 16)
        v = low_v[0, rows, :].astype(F32)
        mean_sq = jnp.sum(v * v, axis=1, keepdims=True) * (1.0 / 4096)
        normed[rows, :] = (v * lax.rsqrt(mean_sq + EPS) * gain).astype(BF16)
        return carry

    lax.fori_loop(0, 2, norm_rows, 0)

    def to(axis, mask):
        return dev(jx=mask) if axis == "x" else dev(jy=mask)

    r2_copies = {}
    for jx in ORDER:
        for b, (axis, m1, m2) in enumerate(ROUTES):
            low = min(m1, 2)
            if axis == "x":
                if jx not in (m1, 2):
                    continue
                slot = m2 if jx == 2 else 0
                for jyh in (1, 0):
                    pair = slice(jyh * 2, jyh * 2 + 2)
                    r1_copies[b, jx, jyh].wait_recv()
                    s_buf[b, slot, pair] = s_buf[b, slot, pair] + r1[b, jx - low, pair]
                    if slot:
                        r2_copies[b, jyh] = send(
                            s_buf.at[b, m2, pair], r2.at[b, pair], to(axis, m2)
                        )
            else:
                r1_copies[b, jx].wait_recv()
                s_buf[b, m2, jx] = s_buf[b, m2, jx] + r1[b, 2 - low, jx]
                r2_copies[b, jx] = send(s_buf.at[b, m2, jx], r2.at[b, jx], to(axis, m2))
                s_buf[b, 0, jx] = s_buf[b, 0, jx] + r1[b, m1 - low, jx]

    cc[2].wait_recv()
    cs[3] = cs[2] + cr[2]
    cc.append(send(cs.at[3], cr.at[3], dev(jy=2)))
    share(2)
    pass_on(1)
    pass_on(3)
    pl.semaphore_wait(far_sem.at[1], 2)
    far_signal(2)
    lax.fori_loop(2, 5, norm_rows, 0)

    r3_copies = {}

    def forward(b, s, other, m1):
        s_buf[b, 0, s] = s_buf[b, 0, s] + r2[b, s]
        if s in (m1, 2):
            r3_copies[b, s] = send(s_buf.at[b, 0, s], r3.at[b, s - min(m1, 2)], to(other, m1))

    for jx in ORDER:
        for b, (axis, m1, m2) in enumerate(ROUTES):
            if axis == "y":
                r2_copies[b, jx].wait_recv()
                forward(b, jx, "x", m1)
            elif jx in (2, 1):
                jyh = jx - 1
                r2_copies[b, jyh].wait_recv()
                for s in (2, 3) if jyh else (1, 0):
                    forward(b, s, "y", m1)

    pass_on(2)
    lax.fori_loop(5, 8, norm_rows, 0)
    nb = send(normed.at[0:128], normed.at[128:256], dev(other=True))

    cc[3].wait_recv()
    counts = (cs[3] + cr[3])[0:1]
    start = jnp.sum(jnp.where(lane_f == id_col, counts, 0.0), axis=1, keepdims=True)
    first_token = (node * 128).astype(F32)
    token = lax.broadcasted_iota(jnp.int32, (128, 1), 0).astype(F32)
    positions = token + first_token - start
    ld_freq.wait()
    angle = positions * freq_v[...]
    trig[0] = jnp.cos(angle)
    trig[1] = jnp.where(lane < 64, -1.0, 1.0) * jnp.sin(angle)

    r4_copies = []
    for b, (axis, m1, m2) in enumerate(ROUTES):
        other = "y" if axis == "x" else "x"
        low = min(m1, 2)
        r3_copies[b, 2].wait_recv()
        s_buf[b, 0, m2] = s_buf[b, 0, m2] + r3[b, 2 - low]
        r4_copies.append(send(s_buf.at[b, 0, m2], r4.at[b], to(other, m2)))
        r3_copies[b, m1].wait_recv()
        s_buf[b, 0, 0] = s_buf[b, 0, 0] + r3[b, m1 - low]

    z1_copies = []
    for b in (1, 2, 3):
        r4_copies[b].wait_recv()
        s_buf[b, 0, 0] = s_buf[b, 0, 0] + r4[b]
        z1_copies.append(send(s_buf.at[b, 0, 0], z1.at[b - 1], dev(dz=(0, 1, 2, -1)[b])))
    r4_copies[0].wait_recv()
    kept = s_buf[0, 0, 0].astype(F32) + r4[0].astype(F32)

    def project(jp):
        for jyh in range(2):
            for jx in range(4):
                owner = (yh + jyh - 2 * yh * jyh) * 8 + flip(x, jx) * 2
                half = par if jp == 0 else 1 - par
                lhs = jnp.concatenate(
                    [
                        normed[:, pl.ds(pl.multiple_of((owner + s) * 256 + half * 128, 128), 128)]
                        for s in range(2)
                    ],
                    axis=1,
                )
                part = jnp.dot(lhs, wg[jp, jyh, jx].reshape(256, 256), preferred_element_type=F32)
                if jp == 0 and jyh == 0 and jx == 0:
                    acc[...] = part
                else:
                    acc[...] += part

    for copy in z1_copies:
        copy.wait_recv()
    kept = kept + z1[0].astype(F32) + z1[1].astype(F32)
    late = z1[2].astype(F32)
    kept = kept + jnp.concatenate([late[7:8], late[0:7]], axis=0)
    zs[...] = kept.astype(BF16)
    pl.semaphore_wait(far_sem.at[2], 2)
    z2_copies = {a: send(zs.at[a], z2.at[a - 1], dev(dz=4 * a)) for a in (4, 3, 5, 2, 6, 1, 7)}

    nb.wait_recv()
    project(0)
    for copy in w5:
        copy.wait_recv()
    project(1)
    kx = send(acc.at[128:256], kr, dev(other=True))

    def rotate(source, half):
        for h in range(2):
            k = source[0:128, h * 128:(h + 1) * 128]
            turned = k * trig[0] + pltpu.roll(k, 64, 1) * trig[1]
            lanes = pl.ds(pl.multiple_of(half * 256 + h * 128, 128), 128)
            keys_ref[:, lanes] = turned.astype(BF16)

    rotate(acc, c)
    kx.wait_recv()
    rotate(kr, 1 - c)

    total = kept[0]
    for a in range(1, 8):
        z2_copies[a].wait_recv()
        total = total + z2[a - 1].astype(F32)
    grad_ref[...] = total

    for copy in sent:
        copy.wait_send()


def fused(x_this, grad_values, x_lower, gain, weight_lower, ids, freq):
    tiles = (8, 16, 128)
    anywhere = pl.BlockSpec(memory_space=pl.ANY)
    vmem = pl.BlockSpec(memory_space=pltpu.VMEM)
    return pl.pallas_call(
        kernel,
        out_shape=(
            jax.ShapeDtypeStruct((16, 128), F32),
            jax.ShapeDtypeStruct((128, 512), BF16),
        ),
        in_specs=[anywhere] * 7,
        out_specs=(vmem, vmem),
        scratch_shapes=[
            pltpu.VMEM((1, 128, 4096), BF16),
            pltpu.VMEM((1, 128, 512), BF16),
            pltpu.VMEM((1, 128, 4096), BF16),
            pltpu.VMEM((1, 4096), F32),
            pltpu.VMEM((256, 512), BF16),
            pltpu.VMEM((1, 128), jnp.int32),
            pltpu.VMEM((1, 128), F32),
            pltpu.VMEM((32, 2, 8, 128), F32),
            pltpu.VMEM((1024, 128), BF16),
            pltpu.VMEM((4, 2, 4, 2) + tiles, BF16),
            pltpu.VMEM((4, 2, 4, 2) + tiles, BF16),
            pltpu.VMEM((4, 4, 4) + tiles, BF16),
            pltpu.VMEM((4, 2, 4) + tiles, BF16),
            pltpu.VMEM((4, 4) + tiles, BF16),
            pltpu.VMEM((4, 2) + tiles, BF16),
            pltpu.VMEM((4,) + tiles, BF16),
            pltpu.VMEM((3,) + tiles, BF16),
            pltpu.VMEM((7, 16, 128), BF16),
            pltpu.VMEM(tiles, BF16),
            pltpu.VMEM((2, 2, 4, 2, 128, 256), BF16),
            pltpu.VMEM((256, 4096), BF16),
            pltpu.VMEM((256, 256), F32),
            pltpu.VMEM((128, 256), F32),
            pltpu.VMEM((4, 8, 128), F32),
            pltpu.VMEM((4, 8, 128), F32),
            pltpu.VMEM((2, 128, 128), F32),
            pltpu.SemaphoreType.DMA((7,)),
            pltpu.SemaphoreType.DMA((N_SEM,)),
            pltpu.SemaphoreType.DMA((N_SEM,)),
            pltpu.SemaphoreType.REGULAR((3,)),
        ],
        compiler_params=pltpu.CompilerParams(
            collective_id=0, has_side_effects=True, vmem_limit_bytes=60 * 1024 * 1024
        ),
        cost_estimate=pl.CostEstimate(
            flops=2 * 2 * 128 * 4096 * 512, bytes_accessed=4 * 1024 * 1024, transcendentals=32768
        ),
    )(x_this, grad_values, x_lower, gain, weight_lower, ids, freq)


def on_device(x_this, grad_values, x_lower, norm_gain, weight_lower, segment_ids):
    exponent = np.arange(128) % 64 * 2.0 / 128
    freq = jnp.asarray((500000.0 ** (-exponent)).astype(np.float32)[None])
    grad, keys = fused(
        x_this, grad_values, x_lower, norm_gain[None], weight_lower, segment_ids, freq
    )
    grad = grad.reshape(2, 8, 128).transpose(0, 2, 1).reshape(256, 8)
    return (grad, keys[None])


def solution(mesh):
    return jax.shard_map(
        on_device,
        mesh=mesh,
        in_specs=(
            P("dp", "node", None),
            P("dp", "node", None),
            P("dp", "node", None),
            P(),
            P("node", None),
            P("dp", "node"),
        ),
        out_specs=(P("node", "dp"), P("dp", "node", None)),
        check_vma=False,
    )
```

time: 87.5 us -> 70.7 us (0.81)
  the two profiles are of different devices: /device:TPU:8 before, /device:TPU:32 now
where the time goes in v2:
time: 70.7 us; the launch traced here: 70.5 us
  Pallas kernels  67 us (95%)
  local copies, waits for them, and re-layouts  2.86 us (4%)
    pallas_call x1, Pallas kernels, fused(): pl.pallas_call(kernel, out_shape=(jax.ShapeDtypeStruct((16, 128), F32), j...  67 us
    unnamed x2, local copies, waits for them, and re-layouts  2.86 us

profile of v2, /device:TPU:32, one launch (start us, length us, event | category | flops | bytes accessed | tf_op | source)
XLA Modules:
  0.0 70.5 jit_solution(12991313753541708020)
XLA Ops:
  0.6 67.0 %shard_map.86 = (f32[16,128]{1,0:T(8,128)}, bf16[128,512]{1,0:T(8,128)(2,1)}) custom-call(bf16[1,128,4096]{2,1,0:T(8,128)(2,1)} %x_hbm.1, bf16[1,128,512]{2,1,0:T(8,128)(2,1)} %g_hbm.1, bf16[1,128,4096]{2,1,0:T(8,128)(2,1)} %low_hbm.1, f32[1,4096]{1,0:T(1,128)} %bitcast.9, bf16[256,512]{1,0:T(8,128)(2,1)} %w_hbm.1, s32[1,128]{1,0:T(1,128)} %ids_hbm.1, ...), custom_call_target="tpu_custom_call" | custom-call | flops 1073741824 | bytes 4194304 | tf_op jit(solution)/shard_map/pallas_call | solution.py:371
  67.6 1.3 %copy.11 = f32[256,8]{0,1:T(8,128)} copy(f32[256,8]{0,1:T(8,128)} %bitcast.8) | data formatting | bytes 16384
  68.9 1.6 %copy.12 = bf16[1,128,512]{2,1,0:T(8,128)(2,1)} copy(bf16[1,128,512]{2,1,0:T(8,128)(2,1)} %bitcast.7) | data formatting | bytes 262144

commit v3 on v2

--- a/solution.py
+++ b/solution.py
@@ -107,6 +107,15 @@
 
         return piece
 
+    def sibling_terms(jx):
+        for jyh in (1, 0):
+            piece = term(jx, jyh, 1 - c)
+            for b in range(4):
+                for jl in range(2):
+                    c_send[jx, jyh, b, jl] = piece(b, jl).astype(BF16)
+
+    ld_x.wait()
+    sibling_terms(2)
     ld_w.wait()
     rows = pl.ds(pl.multiple_of(par * 128, 128), 128)
     away = pl.ds(pl.multiple_of((1 - c) * 256, 256), 256)
@@ -124,30 +133,35 @@
     cc = [send(cs.at[0], cr.at[0], dev(other=True))]
     w3, w4, w5 = {}, {}, []
 
-    def spread(jx):
-        w3[jx] = send(wg.at[0, 0, jx, 1 - yl], wg.at[0, 1, jx, 1 - yl], dev(jy=3))
-        w5.append(send(wg.at[0, 0, jx, 0], wg.at[1, 0, jx, 0], dev(dz=1)))
-        w5.append(send(wg.at[0, 0, jx, 1], wg.at[1, 0, jx, 1], dev(dz=-1)))
-
-    def share(jx):
-        w3[jx].wait_recv()
-        w4[jx] = send(wg.at[0, 1, jx, yl], wg.at[0, 1, jx, yl], dev(jy=1))
-        w5.append(send(wg.at[0, 1, jx, yl], wg.at[1, 1, jx, yl], dev(dz=1 - 2 * yl)))
-
-    def pass_on(jx):
-        w4[jx].wait_recv()
-        w5.append(send(wg.at[0, 1, jx, 1 - yl], wg.at[1, 1, jx, 1 - yl], dev(dz=2 * yl - 1)))
-
-    ld_x.wait()
+    groups = (slice(0, 1), slice(1, 3), slice(3, 4))
+
+    def spread_y(k):
+        part = wg.at[0, 0, groups[k], 1 - yl]
+        w3[k] = send(part, wg.at[0, 1, groups[k], 1 - yl], dev(jy=3))
+
+    def spread_z(k):
+        for core, dz in ((0, 1), (1, -1)):
+            part = wg.at[0, 0, groups[k], core]
+            w5.append(send(part, wg.at[1, 0, groups[k], core], dev(dz=dz)))
+
+    def share(k):
+        w3[k].wait_recv()
+        part = wg.at[0, 1, groups[k], yl]
+        w4[k] = send(part, wg.at[0, 1, groups[k], yl], dev(jy=1))
+        w5.append(send(part, wg.at[1, 1, groups[k], yl], dev(dz=1 - 2 * yl)))
+
+    def pass_on(k):
+        w4[k].wait_recv()
+        part = wg.at[0, 1, groups[k], 1 - yl]
+        w5.append(send(part, wg.at[1, 1, groups[k], 1 - yl], dev(dz=2 * yl - 1)))
+
     c_copies = {}
     r1_copies = {}
 
     def for_sibling(jx):
+        if jx != 2:
+            sibling_terms(jx)
         for jyh in (1, 0):
-            piece = term(jx, jyh, 1 - c)
-            for b in range(4):
-                for jl in range(2):
-                    c_send[jx, jyh, b, jl] = piece(b, jl).astype(BF16)
             c_copies[jx, jyh] = send(c_send.at[jx, jyh], c_recv.at[jx, jyh], dev(other=True))
 
     def own(jx):
@@ -178,37 +192,22 @@
 
     for_sibling(2)
     for_sibling(1)
+    own(2)
     w0.wait_recv()
     w1a = send(wg.at[0, 0, 0], wg.at[0, 0, 1], dev(jx=1))
-    w1b = send(wg.at[0, 0, 0], wg.at[0, 0, 3], dev(jx=3))
-    spread(0)
-    own(2)
+    w1b = send(wg.at[0, 0, 0], wg.at[0, 0, 2], dev(jx=3))
+    spread_y(0)
+    spread_z(0)
     for_sibling(3)
     own(1)
     cc[0].wait_recv()
     cs[1] = cs[0] + cr[0]
     cc.append(send(cs.at[1], cr.at[1], dev(jx=1)))
-    w1a.wait_recv()
-    w1b.wait_recv()
-    w2a = send(wg.at[0, 0, 3, 0], wg.at[0, 0, 2, 0], dev(jx=1))
-    w2b = send(wg.at[0, 0, 1, 1], wg.at[0, 0, 2, 1], dev(jx=3))
-    spread(1)
-    spread(3)
     for_sibling(0)
     own(3)
-    share(0)
+    own(0)
     pl.semaphore_wait(far_sem.at[0], 2)
     far_signal(1)
-    own(0)
-    cc[1].wait_recv()
-    cs[2] = cs[1] + cr[1]
-    cc.append(send(cs.at[2], cr.at[2], dev(jx=3)))
-    w2a.wait_recv()
-    w2b.wait_recv()
-    spread(2)
-    share(1)
-    pass_on(0)
-    share(3)
 
     ld_low.wait()
     ld_gain.wait()
@@ -248,14 +247,16 @@
                 r2_copies[b, jx] = send(s_buf.at[b, m2, jx], r2.at[b, jx], to(axis, m2))
                 s_buf[b, 0, jx] = s_buf[b, 0, jx] + r1[b, m1 - low, jx]
 
-    cc[2].wait_recv()
-    cs[3] = cs[2] + cr[2]
-    cc.append(send(cs.at[3], cr.at[3], dev(jy=2)))
-    share(2)
-    pass_on(1)
-    pass_on(3)
-    pl.semaphore_wait(far_sem.at[1], 2)
-    far_signal(2)
+    cc[1].wait_recv()
+    cs[2] = cs[1] + cr[1]
+    cc.append(send(cs.at[2], cr.at[2], dev(jx=3)))
+    w1a.wait_recv()
+    w1b.wait_recv()
+    w2a = send(wg.at[0, 0, 2, 0], wg.at[0, 0, 3, 0], dev(jx=1))
+    w2b = send(wg.at[0, 0, 1, 1], wg.at[0, 0, 3, 1], dev(jx=3))
+    spread_y(1)
+    spread_z(1)
+    share(0)
     lax.fori_loop(2, 5, norm_rows, 0)
 
     r3_copies = {}
@@ -276,9 +277,39 @@
                 for s in (2, 3) if jyh else (1, 0):
                     forward(b, s, "y", m1)
 
-    pass_on(2)
+    cc[2].wait_recv()
+    cs[3] = cs[2] + cr[2]
+    cc.append(send(cs.at[3], cr.at[3], dev(jy=2)))
+    pl.semaphore_wait(far_sem.at[1], 2)
+    far_signal(2)
     lax.fori_loop(5, 8, norm_rows, 0)
     nb = send(normed.at[0:128], normed.at[128:256], dev(other=True))
+
+    pass_on(0)
+
+    r4_copies = []
+    for b, (axis, m1, m2) in enumerate(ROUTES):
+        other = "y" if axis == "x" else "x"
+        low = min(m1, 2)
+        r3_copies[b, 2].wait_recv()
+        s_buf[b, 0, m2] = s_buf[b, 0, m2] + r3[b, 2 - low]
+        r4_copies.append(send(s_buf.at[b, 0, m2], r4.at[b], to(other, m2)))
+        r3_copies[b, m1].wait_recv()
+        s_buf[b, 0, 0] = s_buf[b, 0, 0] + r3[b, m1 - low]
+
+    w2a.wait_recv()
+    w2b.wait_recv()
+    spread_y(2)
+    spread_z(2)
+
+    z1_copies = []
+    for b in (1, 2, 3):
+        r4_copies[b].wait_recv()
+        s_buf[b, 0, 0] = s_buf[b, 0, 0] + r4[b]
+        z1_copies.append(send(s_buf.at[b, 0, 0], z1.at[b - 1], dev(dz=(0, 1, 2, -1)[b])))
+    r4_copies[0].wait_recv()
+    kept = s_buf[0, 0, 0].astype(F32) + r4[0].astype(F32)
+    share(1)
 
     cc[3].wait_recv()
     counts = (cs[3] + cr[3])[0:1]
@@ -291,41 +322,23 @@
     trig[0] = jnp.cos(angle)
     trig[1] = jnp.where(lane < 64, -1.0, 1.0) * jnp.sin(angle)
 
-    r4_copies = []
-    for b, (axis, m1, m2) in enumerate(ROUTES):
-        other = "y" if axis == "x" else "x"
-        low = min(m1, 2)
-        r3_copies[b, 2].wait_recv()
-        s_buf[b, 0, m2] = s_buf[b, 0, m2] + r3[b, 2 - low]
-        r4_copies.append(send(s_buf.at[b, 0, m2], r4.at[b], to(other, m2)))
-        r3_copies[b, m1].wait_recv()
-        s_buf[b, 0, 0] = s_buf[b, 0, 0] + r3[b, m1 - low]
-
-    z1_copies = []
-    for b in (1, 2, 3):
-        r4_copies[b].wait_recv()
-        s_buf[b, 0, 0] = s_buf[b, 0, 0] + r4[b]
-        z1_copies.append(send(s_buf.at[b, 0, 0], z1.at[b - 1], dev(dz=(0, 1, 2, -1)[b])))
-    r4_copies[0].wait_recv()
-    kept = s_buf[0, 0, 0].astype(F32) + r4[0].astype(F32)
-
-    def project(jp):
-        for jyh in range(2):
-            for jx in range(4):
-                owner = (yh + jyh - 2 * yh * jyh) * 8 + flip(x, jx) * 2
-                half = par if jp == 0 else 1 - par
-                lhs = jnp.concatenate(
-                    [
-                        normed[:, pl.ds(pl.multiple_of((owner + s) * 256 + half * 128, 128), 128)]
-                        for s in range(2)
-                    ],
-                    axis=1,
-                )
-                part = jnp.dot(lhs, wg[jp, jyh, jx].reshape(256, 256), preferred_element_type=F32)
-                if jp == 0 and jyh == 0 and jx == 0:
-                    acc[...] = part
-                else:
-                    acc[...] += part
+
+    def project(jp, jyh):
+        for slot, jx in enumerate((0, 1, 3, 2)):
+            owner = (yh + jyh - 2 * yh * jyh) * 8 + flip(x, jx) * 2
+            half = par if jp == 0 else 1 - par
+            lhs = jnp.concatenate(
+                [
+                    normed[:, pl.ds(pl.multiple_of((owner + s) * 256 + half * 128, 128), 128)]
+                    for s in range(2)
+                ],
+                axis=1,
+            )
+            part = jnp.dot(lhs, wg[jp, jyh, slot].reshape(256, 256), preferred_element_type=F32)
+            if jp == 0 and jyh == 0 and jx == 0:
+                acc[...] = part
+            else:
+                acc[...] += part
 
     for copy in z1_copies:
         copy.wait_recv()
@@ -336,11 +349,16 @@
     pl.semaphore_wait(far_sem.at[2], 2)
     z2_copies = {a: send(zs.at[a], z2.at[a - 1], dev(dz=4 * a)) for a in (4, 3, 5, 2, 6, 1, 7)}
 
+    share(2)
+    pass_on(1)
     nb.wait_recv()
-    project(0)
+    project(0, 0)
+    pass_on(2)
+    project(0, 1)
     for copy in w5:
         copy.wait_recv()
-    project(1)
+    project(1, 0)
+    project(1, 1)
     kx = send(acc.at[128:256], kr, dev(other=True))
 
     def rotate(source, half):
@@ -371,8 +389,8 @@
     return pl.pallas_call(
         kernel,
         out_shape=(
-            jax.ShapeDtypeStruct((16, 128), F32),
-            jax.ShapeDtypeStruct((128, 512), BF16),
+            pltpu.VMEM((16, 128), F32),
+            pltpu.VMEM((128, 512), BF16),
         ),
         in_specs=[anywhere] * 7,
         out_specs=(vmem, vmem),

time: 70.7 us -> 67.8 us (0.959)
  the two profiles are of different devices: /device:TPU:32 before, /device:TPU:2 now
where the time goes in v3:
time: 67.8 us; the launch traced here: 67.6 us
  Pallas kernels  65.7 us (97%)
  local copies, waits for them, and re-layouts  1.26 us (2%)
    pallas_call x1, Pallas kernels, fused(): pl.pallas_call(kernel, out_shape=(pltpu.VMEM((16, 128), F32), pltpu.VMEM(...  65.7 us

profile of v3, /device:TPU:2, one launch (start us, length us, event | category | flops | bytes accessed | tf_op | source)
XLA Modules:
  0.0 67.6 jit_solution(1044425850832301722)
XLA Ops:
  0.6 65.7 %shard_map.86 = (f32[16,128]{1,0:T(8,128)S(1)}, bf16[128,512]{1,0:T(8,128)(2,1)S(1)}) custom-call(bf16[1,128,4096]{2,1,0:T(8,128)(2,1)} %x_hbm.1, bf16[1,128,512]{2,1,0:T(8,128)(2,1)} %g_hbm.1, bf16[1,128,4096]{2,1,0:T(8,128)(2,1)} %low_hbm.1, f32[1,4096]{1,0:T(1,128)} %bitcast.9, bf16[256,512]{1,0:T(8,128)(2,1)} %w_hbm.1, s32[1,128]{1,0:T(1,128)} %ids_hbm.1, ...), custom_call_target="tpu_custom_call" | custom-call | flops 1073741824 | bytes 4194304 | tf_op jit(solution)/shard_map/pallas_call | solution.py:389
  66.3 0.6 copy.11
  66.9 0.7 copy.12

commit v4 on v3

--- a/solution.py
+++ b/solution.py
@@ -131,7 +131,7 @@
     far_signal(0)
     w0 = send(w_v.at[rows, away], wg.at[0, 0, 0, c], dev(other=True))
     cc = [send(cs.at[0], cr.at[0], dev(other=True))]
-    w3, w4, w5 = {}, {}, []
+    w3, w4, w5 = {}, {}, ([], [])
 
     groups = (slice(0, 1), slice(1, 3), slice(3, 4))
 
@@ -142,18 +142,18 @@
     def spread_z(k):
         for core, dz in ((0, 1), (1, -1)):
             part = wg.at[0, 0, groups[k], core]
-            w5.append(send(part, wg.at[1, 0, groups[k], core], dev(dz=dz)))
+            w5[0].append(send(part, wg.at[1, 0, groups[k], core], dev(dz=dz)))
 
     def share(k):
         w3[k].wait_recv()
         part = wg.at[0, 1, groups[k], yl]
         w4[k] = send(part, wg.at[0, 1, groups[k], yl], dev(jy=1))
-        w5.append(send(part, wg.at[1, 1, groups[k], yl], dev(dz=1 - 2 * yl)))
+        w5[1].append(send(part, wg.at[1, 1, groups[k], yl], dev(dz=1 - 2 * yl)))
 
     def pass_on(k):
         w4[k].wait_recv()
         part = wg.at[0, 1, groups[k], 1 - yl]
-        w5.append(send(part, wg.at[1, 1, groups[k], 1 - yl], dev(dz=2 * yl - 1)))
+        w5[1].append(send(part, wg.at[1, 1, groups[k], 1 - yl], dev(dz=2 * yl - 1)))
 
     c_copies = {}
     r1_copies = {}
@@ -193,11 +193,6 @@
     for_sibling(2)
     for_sibling(1)
     own(2)
-    w0.wait_recv()
-    w1a = send(wg.at[0, 0, 0], wg.at[0, 0, 1], dev(jx=1))
-    w1b = send(wg.at[0, 0, 0], wg.at[0, 0, 2], dev(jx=3))
-    spread_y(0)
-    spread_z(0)
     for_sibling(3)
     own(1)
     cc[0].wait_recv()
@@ -206,6 +201,11 @@
     for_sibling(0)
     own(3)
     own(0)
+    w0.wait_recv()
+    w1a = send(wg.at[0, 0, 0], wg.at[0, 0, 1], dev(jx=1))
+    w1b = send(wg.at[0, 0, 0], wg.at[0, 0, 2], dev(jx=3))
+    spread_y(0)
+    spread_z(0)
     pl.semaphore_wait(far_sem.at[0], 2)
     far_signal(1)
 
@@ -250,13 +250,6 @@
     cc[1].wait_recv()
     cs[2] = cs[1] + cr[1]
     cc.append(send(cs.at[2], cr.at[2], dev(jx=3)))
-    w1a.wait_recv()
-    w1b.wait_recv()
-    w2a = send(wg.at[0, 0, 2, 0], wg.at[0, 0, 3, 0], dev(jx=1))
-    w2b = send(wg.at[0, 0, 1, 1], wg.at[0, 0, 3, 1], dev(jx=3))
-    spread_y(1)
-    spread_z(1)
-    share(0)
     lax.fori_loop(2, 5, norm_rows, 0)
 
     r3_copies = {}
@@ -285,7 +278,14 @@
     lax.fori_loop(5, 8, norm_rows, 0)
     nb = send(normed.at[0:128], normed.at[128:256], dev(other=True))
 
-    pass_on(0)
+
+    w1a.wait_recv()
+    w1b.wait_recv()
+    w2a = send(wg.at[0, 0, 2, 0], wg.at[0, 0, 3, 0], dev(jx=1))
+    w2b = send(wg.at[0, 0, 1, 1], wg.at[0, 0, 3, 1], dev(jx=3))
+    spread_y(1)
+    spread_z(1)
+    share(0)
 
     r4_copies = []
     for b, (axis, m1, m2) in enumerate(ROUTES):
@@ -297,11 +297,6 @@
         r3_copies[b, m1].wait_recv()
         s_buf[b, 0, 0] = s_buf[b, 0, 0] + r3[b, m1 - low]
 
-    w2a.wait_recv()
-    w2b.wait_recv()
-    spread_y(2)
-    spread_z(2)
-
     z1_copies = []
     for b in (1, 2, 3):
         r4_copies[b].wait_recv()
@@ -309,7 +304,7 @@
         z1_copies.append(send(s_buf.at[b, 0, 0], z1.at[b - 1], dev(dz=(0, 1, 2, -1)[b])))
     r4_copies[0].wait_recv()
     kept = s_buf[0, 0, 0].astype(F32) + r4[0].astype(F32)
-    share(1)
+    pass_on(0)
 
     cc[3].wait_recv()
     counts = (cs[3] + cr[3])[0:1]
@@ -340,6 +335,14 @@
             else:
                 acc[...] += part
 
+    w2a.wait_recv()
+    w2b.wait_recv()
+    spread_y(2)
+    spread_z(2)
+    share(1)
+    nb.wait_recv()
+    project(0, 0)
+
     for copy in z1_copies:
         copy.wait_recv()
     kept = kept + z1[0].astype(F32) + z1[1].astype(F32)
@@ -351,14 +354,12 @@
 
     share(2)
     pass_on(1)
-    nb.wait_recv()
-    project(0, 0)
     pass_on(2)
     project(0, 1)
-    for copy in w5:
-        copy.wait_recv()
-    project(1, 0)
-    project(1, 1)
+    for jyh in range(2):
+        for copy in w5[jyh]:
+            copy.wait_recv()
+        project(1, jyh)
     kx = send(acc.at[128:256], kr, dev(other=True))
 
     def rotate(source, half):

time: 67.8 us -> 66.2 us (0.976)
  the two profiles are of different devices: /device:TPU:2 before, /device:TPU:1 now
where the time goes in v4:
time: 66.2 us; the launch traced here: 66.1 us
  Pallas kernels  64.2 us (97%)
  local copies, waits for them, and re-layouts  1.26 us (2%)
    pallas_call x1, Pallas kernels, fused(): pl.pallas_call(kernel, out_shape=(pltpu.VMEM((16, 128), F32), pltpu.VMEM(...  64.2 us

profile of v4, /device:TPU:1, one launch (start us, length us, event | category | flops | bytes accessed | tf_op | source)
XLA Modules:
  0.0 66.1 jit_solution(9671547766869218789)
XLA Ops:
  0.6 64.2 %shard_map.86 = (f32[16,128]{1,0:T(8,128)S(1)}, bf16[128,512]{1,0:T(8,128)(2,1)S(1)}) custom-call(bf16[1,128,4096]{2,1,0:T(8,128)(2,1)} %x_hbm.1, bf16[1,128,512]{2,1,0:T(8,128)(2,1)} %g_hbm.1, bf16[1,128,4096]{2,1,0:T(8,128)(2,1)} %low_hbm.1, f32[1,4096]{1,0:T(1,128)} %bitcast.9, bf16[256,512]{1,0:T(8,128)(2,1)} %w_hbm.1, s32[1,128]{1,0:T(1,128)} %ids_hbm.1, ...), custom_call_target="tpu_custom_call" | custom-call | flops 1073741824 | bytes 4194304 | tf_op jit(solution)/shard_map/pallas_call | solution.py:390
  64.8 0.6 copy.11
  65.4 0.7 copy.12

commit v5 on v4

--- a/solution.py
+++ b/solution.py
@@ -206,8 +206,6 @@
     w1b = send(wg.at[0, 0, 0], wg.at[0, 0, 2], dev(jx=3))
     spread_y(0)
     spread_z(0)
-    pl.semaphore_wait(far_sem.at[0], 2)
-    far_signal(1)
 
     ld_low.wait()
     ld_gain.wait()
@@ -250,6 +248,8 @@
     cc[1].wait_recv()
     cs[2] = cs[1] + cr[1]
     cc.append(send(cs.at[2], cr.at[2], dev(jx=3)))
+    pl.semaphore_wait(far_sem.at[0], 2)
+    far_signal(1)
     lax.fori_loop(2, 5, norm_rows, 0)
 
     r3_copies = {}
@@ -273,8 +273,6 @@
     cc[2].wait_recv()
     cs[3] = cs[2] + cr[2]
     cc.append(send(cs.at[3], cr.at[3], dev(jy=2)))
-    pl.semaphore_wait(far_sem.at[1], 2)
-    far_signal(2)
     lax.fori_loop(5, 8, norm_rows, 0)
     nb = send(normed.at[0:128], normed.at[128:256], dev(other=True))
 
@@ -296,6 +294,9 @@
         r4_copies.append(send(s_buf.at[b, 0, m2], r4.at[b], to(other, m2)))
         r3_copies[b, m1].wait_recv()
         s_buf[b, 0, 0] = s_buf[b, 0, 0] + r3[b, m1 - low]
+
+    pl.semaphore_wait(far_sem.at[1], 2)
+    far_signal(2)
 
     z1_copies = []
     for b in (1, 2, 3):

time: 66.2 us -> 66 us (level)
  the two profiles are of different devices: /device:TPU:1 before, /device:TPU:2 now
where the time goes in v5:
time: 66 us; the launch traced here: 65.9 us
  Pallas kernels  64 us (97%)
  local copies, waits for them, and re-layouts  1.26 us (2%)
    pallas_call x1, Pallas kernels, fused(): pl.pallas_call(kernel, out_shape=(pltpu.VMEM((16, 128), F32), pltpu.VMEM(...  64 us

profile of v5, /device:TPU:2, one launch (start us, length us, event | category | flops | bytes accessed | tf_op | source)
XLA Modules:
  0.0 65.9 jit_solution(1870142362296248081)
XLA Ops:
  0.6 64.0 %shard_map.86 = (f32[16,128]{1,0:T(8,128)S(1)}, bf16[128,512]{1,0:T(8,128)(2,1)S(1)}) custom-call(bf16[1,128,4096]{2,1,0:T(8,128)(2,1)} %x_hbm.1, bf16[1,128,512]{2,1,0:T(8,128)(2,1)} %g_hbm.1, bf16[1,128,4096]{2,1,0:T(8,128)(2,1)} %low_hbm.1, f32[1,4096]{1,0:T(1,128)} %bitcast.9, bf16[256,512]{1,0:T(8,128)(2,1)} %w_hbm.1, s32[1,128]{1,0:T(1,128)} %ids_hbm.1, ...), custom_call_target="tpu_custom_call" | custom-call | flops 1073741824 | bytes 4194304 | tf_op jit(solution)/shard_map/pallas_call | solution.py:391
  64.6 0.6 copy.11
  65.2 0.7 copy.12
